TPU v7x, 128 devices: a whole 4x4x4 slice. The times are simulated.
128 devices in a mesh: dp: 16 (over z_hi, x, core), tensor: 8 (over z_lo, y).
Axes of the slice: x: 4, y: 4, z: 4 (z_hi: 2, z_lo: 2; z = z_hi * 2 + z_lo), core: 2. Of those that a mesh axis runs over, the one named last changes fastest.
Arguments:
- teacher_states: bfloat16 [3, 2048, 2, 8192], P(None, 'dp', None, 'tensor'), may hold values from -8 to 8
- student_states: bfloat16 [3, 2048, 2, 3072], P(None, 'dp', None, 'tensor'), may hold values from -8 to 8
Outputs:
- relation_loss: float32 [], replicated
- student_grads: bfloat16 [3, 2048, 2, 3072], P(None, 'dp', None, 'tensor')
All inputs are finite; a program needn't handle non-finite values.
Results may differ from a plain program's by a relative error of at most 0.0047.
Values may be sent and summed in bfloat16 or wider, within the bound.
A program may use at most 192 MiB of HBM per device.

v0:
```python
import functools
import math

import jax
import jax.numpy as jnp
from jax import lax
from jax.experimental import pallas as pl
from jax.experimental.pallas import tpu as pltpu
from jax.sharding import PartitionSpec as P

RELATIONS = 3
SEQS = 2
RH = 64
LENGTH = 2048
TW = 128
SW = 48
DP = 16
TENSOR = 8
ROWS = LENGTH // DP
HEADS = RH // TENSOR
BLOCK = 256
CHUNK = 256
LOSS_SCALE = 16.0
LOG2E = 1.0 / math.log(2.0)
T_SCALE = LOG2E / math.sqrt(TW)
S_SCALE = LOG2E / math.sqrt(SW)
MESH = pl.DeviceIdType.MESH
f32 = jnp.float32
bf16 = jnp.bfloat16


def dot_nt(a, b):
    return lax.dot_general(a, b, (((1,), (1,)), ((), ())), preferred_element_type=f32)


def dot_nn(a, b):
    return jnp.dot(a, b, preferred_element_type=f32)


def prepare(teacher, student, t_left, t_right, s_left, s_right, s_feat):
    norms = []
    largest = jnp.zeros((1, ROWS), f32)
    for p in range(DP):
        x = student[p].astype(f32)
        square = jnp.sum(x * x, axis=0, keepdims=True)
        norms.append(square)
        largest = jnp.maximum(largest, square)
    largest = jnp.max(largest, axis=1, keepdims=True)
    first = lax.broadcasted_iota(jnp.int32, (16, ROWS), 0) == 0
    ones = jnp.where(first, 1.0, 0.0)
    zeros = jnp.zeros((16, ROWS), f32)
    for p in range(DP):
        rows = slice(p * ROWS, (p + 1) * ROWS)
        x = student[p].astype(f32)
        scaled = x * S_SCALE
        high = scaled.astype(bf16)
        low = (scaled - high.astype(f32)).astype(bf16)
        shift = (0.5 * S_SCALE) * (jnp.sqrt(norms[p] * largest) + norms[p])
        shift = jnp.where(first, -shift, 0.0).astype(bf16)
        s_right[:, rows] = jnp.concatenate([high, low, shift, zeros.astype(bf16)], axis=0)
        s_left[rows, :] = jnp.concatenate([x, x, ones, zeros], axis=0).T.astype(bf16)
        s_feat[:, rows] = student[p]
        x = teacher[p]
        scaled = x.astype(f32) * T_SCALE
        high = scaled.astype(bf16)
        t_left[rows, 0:TW] = x
        t_left[rows, TW:] = x
        t_right[rows, 0:TW] = high
        t_right[rows, TW:] = (scaled - high.astype(f32)).astype(bf16)


def score_block(i, t_left, t_right, s_left, s_right, s_feat, t_exp, s_exp, total, kl):
    own = pl.ds(pl.multiple_of(i * BLOCK, BLOCK), BLOCK)
    t_own = t_right[own, :]
    s_own = s_right[:, own]
    count = LENGTH // CHUNK
    t_max, t_sum, cross = [], [], []
    s_sum = jnp.zeros((1, BLOCK), f32)
    for k in range(count):
        part = slice(k * CHUNK, (k + 1) * CHUNK)
        t = dot_nt(t_left[part, :], t_own)
        top = jnp.max(t, axis=0, keepdims=True)
        t = t - top
        s = dot_nn(s_left[part, :], s_own)
        te = jnp.exp2(t)
        se = jnp.exp2(s)
        t_max.append(top)
        t_sum.append(jnp.sum(te, axis=0, keepdims=True))
        cross.append(jnp.sum(te * (t - s), axis=0, keepdims=True))
        s_sum = s_sum + jnp.sum(se, axis=0, keepdims=True)
        t_exp[part, :] = te
        s_exp[part, :] = se
    top = functools.reduce(jnp.maximum, t_max)
    lift = [jnp.exp2(x - top) for x in t_max]
    z = sum(f * x for f, x in zip(lift, t_sum))
    cross = sum(f * (c + (m - top) * x) for f, c, m, x in zip(lift, cross, t_max, t_sum))
    kl[...] += math.log(2.0) * cross / z - jnp.log(z) + jnp.log(s_sum)
    s_gain = LOSS_SCALE / s_sum
    t_gain = LOSS_SCALE / z
    x_own = s_feat[:, own]
    forward = jnp.zeros((SW, BLOCK), f32)
    for k in range(count):
        part = slice(k * CHUNK, (k + 1) * CHUNK)
        grad = (s_exp[part, :] * s_gain - t_exp[part, :] * (t_gain * lift[k])).astype(bf16)
        forward = forward + dot_nn(s_feat[:, part], grad)
        total[:, part] += dot_nt(x_own, grad)
    total[:, own] += forward


def kernel(
    teacher_hbm, student_hbm, loss_out, grads_out,
    t_in, s_in, t_send, s_send, t_got, s_got, g_send, g_got,
    t_left, t_right, s_left, s_right, s_feat, t_exp, s_exp, total, kl,
    loss_a, loss_b,
    load_sem, t_send_sem, s_send_sem, g_send_sem, t_got_sem, s_got_sem, g_got_sem, loss_send_sem, loss_got_sem,
):
    me = lax.axis_index("dp")
    lane = lax.axis_index("tensor")

    def loads(r):
        return (
            pltpu.make_async_copy(teacher_hbm.at[r], t_in.at[r], load_sem.at[0, r]),
            pltpu.make_async_copy(student_hbm.at[r], s_in.at[r], load_sem.at[1, r]),
        )

    for r in range(RELATIONS):
        for copy in loads(r):
            copy.start()

    barrier = pltpu.get_barrier_semaphore()

    def greet_dp(n, carry):
        pl.semaphore_signal(barrier, inc=1, device_id={"dp": lax.rem(me + n, DP)}, device_id_type=MESH)
        return carry

    def greet_tensor(n, carry):
        pl.semaphore_signal(barrier, inc=1, device_id={"tensor": lax.rem(lane + n, TENSOR)}, device_id_type=MESH)
        return carry

    lax.fori_loop(1, DP, greet_dp, 0)
    lax.fori_loop(1, TENSOR, greet_tensor, 0)

    def pack(r):
        for copy in loads(r):
            copy.wait()
        for s in range(SEQS):
            x = s_in[r, :, s, :].astype(f32).T.astype(bf16)
            for a in range(HEADS):
                s_send[r, s * HEADS + a] = x[a * SW : (a + 1) * SW, :]
            x = t_in[r, :, s, :]
            for a in range(HEADS):
                t_send[r, s * HEADS + a] = x[:, a * TW : (a + 1) * TW]

    def send_blocks(source, target, send_sem, got_sem, r):
        def one(n, carry):
            to = lax.rem(me + n, DP)
            pltpu.make_async_remote_copy(
                src_ref=source.at[r, to],
                dst_ref=target.at[r, me],
                send_sem=send_sem.at[r],
                recv_sem=got_sem.at[r],
                device_id={"dp": to},
                device_id_type=MESH,
            ).start()
            return carry

        lax.fori_loop(1, DP, one, 0)
        target[r, me] = source[r, me]

    def wait_blocks(buffer, sem, r):
        span = buffer.at[r, pl.ds(0, DP - 1)]
        pltpu.make_async_copy(span, span, sem.at[r]).wait()

    def send_inputs(r):
        send_blocks(s_send, s_got, s_send_sem, s_got_sem, r)
        send_blocks(t_send, t_got, t_send_sem, t_got_sem, r)

    def place(r):
        wait_blocks(g_got, g_got_sem, r)
        for s in range(SEQS):
            x = g_got[r, s * HEADS : (s + 1) * HEADS].reshape(HEADS * SW, ROWS)
            grads_out[r, :, s, :] = x.T

    pack(0)
    pl.semaphore_wait(barrier, DP - 1 + TENSOR - 1)
    send_inputs(0)
    pack(1)
    pack(2)
    kl[...] = jnp.zeros_like(kl)

    def relation(r, carry):
        wait_blocks(s_got, s_got_sem, r)
        wait_blocks(t_got, t_got_sem, r)

        @pl.when(r < RELATIONS - 1)
        def _():
            send_inputs(r + 1)

        prepare(t_got.at[r], s_got.at[r], t_left, t_right, s_left, s_right, s_feat)
        total[...] = jnp.zeros_like(total)

        def step(i, inner):
            score_block(i, t_left, t_right, s_left, s_right, s_feat, t_exp, s_exp, total, kl)
            return inner

        lax.fori_loop(0, LENGTH // BLOCK, step, 0)
        for p in range(DP):
            g_send[r, p] = (total[:, p * ROWS : (p + 1) * ROWS] * (1.0 / math.sqrt(SW))).astype(bf16)
        send_blocks(g_send, g_got, g_send_sem, g_got_sem, r)

        @pl.when(r > 0)
        def _():
            place(r - 1)

        return carry

    lax.fori_loop(0, RELATIONS, relation, 0)

    def share(buffer, axis, here, size, which, value):
        buffer[here] = value

        def one(n, carry):
            to = lax.rem(here + n, size)
            pltpu.make_async_remote_copy(
                src_ref=buffer.at[here],
                dst_ref=buffer.at[here],
                send_sem=loss_send_sem.at[which],
                recv_sem=loss_got_sem.at[which],
                device_id={axis: to},
                device_id_type=MESH,
            ).start()
            return carry

        lax.fori_loop(1, size, one, 0)
        span = buffer.at[pl.ds(0, size - 1)]
        pltpu.make_async_copy(span, span, loss_got_sem.at[which]).wait()
        return functools.reduce(lambda a, b: a + b, [buffer[n] for n in range(size)])

    part = jnp.broadcast_to(jnp.sum(kl[...], axis=1, keepdims=True), (8, 128))
    part = share(loss_a, "dp", me, DP, 0, part)
    part = share(loss_b, "tensor", lane, TENSOR, 1, part)
    loss_out[...] = part * (1.0 / (RELATIONS * SEQS * RH * LENGTH))
    place(RELATIONS - 1)

    for r in range(RELATIONS):
        wait_blocks(t_send, t_send_sem, r)
        wait_blocks(s_send, s_send_sem, r)
        wait_blocks(g_send, g_send_sem, r)
    for which, buffer, size in ((0, loss_a, DP), (1, loss_b, TENSOR)):
        span = buffer.at[pl.ds(0, size - 1)]
        pltpu.make_async_copy(span, span, loss_send_sem.at[which]).wait()


def per_device(teacher_states, student_states):
    dma = pltpu.SemaphoreType.DMA
    loss, grads = pl.pallas_call(
        kernel,
        out_shape=(
            jax.ShapeDtypeStruct((8, 128), f32),
            jax.ShapeDtypeStruct(student_states.shape, bf16),
        ),
        in_specs=[pl.BlockSpec(memory_space=pl.ANY)] * 2,
        out_specs=(pl.BlockSpec(memory_space=pltpu.VMEM), pl.BlockSpec(memory_space=pltpu.VMEM)),
        scratch_shapes=[
            pltpu.VMEM((RELATIONS, ROWS, SEQS, HEADS * TW), bf16),
            pltpu.VMEM((RELATIONS, ROWS, SEQS, HEADS * SW), bf16),
            pltpu.VMEM((RELATIONS, DP, ROWS, TW), bf16),
            pltpu.VMEM((RELATIONS, DP, SW, ROWS), bf16),
            pltpu.VMEM((RELATIONS, DP, ROWS, TW), bf16),
            pltpu.VMEM((RELATIONS, DP, SW, ROWS), bf16),
            pltpu.VMEM((RELATIONS, DP, SW, ROWS), bf16),
            pltpu.VMEM((RELATIONS, DP, SW, ROWS), bf16),
            pltpu.VMEM((LENGTH, 2 * TW), bf16),
            pltpu.VMEM((LENGTH, 2 * TW), bf16),
            pltpu.VMEM((LENGTH, 128), bf16),
            pltpu.VMEM((128, LENGTH), bf16),
            pltpu.VMEM((SW, LENGTH), bf16),
            pltpu.VMEM((LENGTH, BLOCK), f32),
            pltpu.VMEM((LENGTH, BLOCK), f32),
            pltpu.VMEM((SW, LENGTH), f32),
            pltpu.VMEM((1, BLOCK), f32),
            pltpu.VMEM((DP, 8, 128), f32),
            pltpu.VMEM((TENSOR, 8, 128), f32),
            dma((2, RELATIONS)),
            dma((RELATIONS,)),
            dma((RELATIONS,)),
            dma((RELATIONS,)),
            dma((RELATIONS,)),
            dma((RELATIONS,)),
            dma((RELATIONS,)),
            dma((2,)),
            dma((2,)),
        ],
        compiler_params=pltpu.CompilerParams(
            collective_id=0, has_side_effects=True, vmem_limit_bytes=48 * 1024 * 1024
        ),
    )(teacher_states, student_states)
    return loss[0, 0], grads


def solution(mesh):
    placed = (P(None, "dp", None, "tensor"), P(None, "dp", None, "tensor"))
    return jax.shard_map(
        per_device,
        mesh=mesh,
        in_specs=placed,
        out_specs=(P(), P(None, "dp", None, "tensor")),
        check_vma=False,
    )
```

profile of v0, /device:TPU:1, one launch (start us, length us, event | category | flops | bytes accessed | tf_op | source)
XLA Modules:
  0.0 80.6 jit_solution(2006073951573619307)
XLA Ops:
  0.6 0.0 copy-start
  0.6 1.4 %copy-done = bf16[3,128,2,1024]{3,2,1,0:T(2,128)(2,1)S(1)} copy-done((bf16[3,128,2,1024]{3,2,1,0:T(2,128)(2,1)S(1)}, bf16[3,128,2,1024]{3,2,1,0:T(2,128)(2,1)}, u32[]{:S(2)}) %copy-start) | copy-done | bytes 1572888
  2.0 0.0 copy-start.1
  2.0 1.1 %copy-done.1 = bf16[3,128,2,384]{3,2,1,0:T(2,128)(2,1)S(1)} copy-done((bf16[3,128,2,384]{3,2,1,0:T(2,128)(2,1)S(1)}, bf16[3,128,2,384]{3,2,1,0:T(2,128)(2,1)}, u32[]{:S(2)}) %copy-start.1) | copy-done | bytes 589848
  3.1 76.1 %shard_map.41 = (f32[8,128]{1,0:T(8,128)S(1)}, bf16[3,128,2,384]{3,2,1,0:T(2,128)(2,1)S(1)}) custom-call(bf16[3,128,2,1024]{3,2,1,0:T(2,128)(2,1)S(1)} %copy-done, bf16[3,128,2,384]{3,2,1,0:T(2,128)(2,1)S(1)} %copy-done.1), custom_call_target="tpu_custom_call" | custom-call | tf_op jit(solution)/shard_map/pallas_call | solution.py:256
  79.2 0.5 slice.3
  79.7 0.8 %copy.5 = bf16[3,128,2,384]{3,2,1,0:T(2,128)(2,1)} copy(bf16[3,128,2,384]{3,2,1,0:T(2,128)(2,1)S(1)} %get-tuple-element.9) | data formatting | bytes 1179648
Async XLA Ops:
  0.6 1.4 %copy-start = (bf16[3,128,2,1024]{3,2,1,0:T(2,128)(2,1)S(1)}, bf16[3,128,2,1024]{3,2,1,0:T(2,128)(2,1)}, u32[]{:S(2)}) copy-start(bf16[3,128,2,1024]{3,2,1,0:T(2,128)(2,1)} %teacher_hbm.1) | copy-start | bytes 4718596
  2.0 1.1 %copy-start.1 = (bf16[3,128,2,384]{3,2,1,0:T(2,128)(2,1)S(1)}, bf16[3,128,2,384]{3,2,1,0:T(2,128)(2,1)}, u32[]{:S(2)}) copy-start(bf16[3,128,2,384]{3,2,1,0:T(2,128)(2,1)} %student_hbm.1) | copy-start | bytes 1769476
where the time goes:
time: 80.7 us; the launch traced here: 80.6 us
  Pallas kernels  76.1 us (94%)
  local copies, waits for them, and re-layouts  3.79 us (5%)
    pallas_call x1, Pallas kernels, per_device(): pl.pallas_call(kernel, out_shape=(jax.ShapeDtypeStruct((8, 128), f32), ja...  76.1 us
    unnamed x5, local copies, waits for them, and re-layouts  3.28 us

commit v1 on v0

--- a/solution.py
+++ b/solution.py
@@ -20,6 +20,7 @@
 HEADS = RH // TENSOR
 BLOCK = 256
 CHUNK = 256
+PIECE = 32
 LOSS_SCALE = 16.0
 LOG2E = 1.0 / math.log(2.0)
 T_SCALE = LOG2E / math.sqrt(TW)
@@ -69,48 +70,80 @@
         t_right[rows, TW:] = (scaled - high.astype(f32)).astype(bf16)
 
 
-def score_block(i, t_left, t_right, s_left, s_right, s_feat, t_exp, s_exp, total, kl):
-    own = pl.ds(pl.multiple_of(i * BLOCK, BLOCK), BLOCK)
-    t_own = t_right[own, :]
-    s_own = s_right[:, own]
+def fold(x, op):
+    parts = [x[8 * n : 8 * n + 8, :] for n in range(x.shape[0] // 8)]
+    while len(parts) > 1:
+        parts = [op(*parts[n : n + 2]) if n + 1 < len(parts) else parts[n] for n in range(0, len(parts), 2)]
+    return parts[0]
+
+
+def score_step(i, now, before, t_left, t_right, s_left, s_right, s_feat, t_exp, s_exp, gain, total, kl):
     count = LENGTH // CHUNK
-    t_max, t_sum, cross = [], [], []
-    s_sum = jnp.zeros((1, BLOCK), f32)
+    repeat = PIECE // 8
+    if before:
+        last = pl.ds(pl.multiple_of((i - 1) * BLOCK, BLOCK), BLOCK)
+        x_last = s_feat[:, last]
+        s_gain = jnp.concatenate([gain[count * 8 :, :]] * repeat, axis=0)
+        t_gain = [gain[k * 8 : k * 8 + 8, :] for k in range(count)]
+        forward = jnp.zeros((SW, BLOCK), f32)
+    if now:
+        own = pl.ds(pl.multiple_of(i * BLOCK, BLOCK), BLOCK)
+        t_own = t_right[own, :]
+        s_own = s_right[:, own]
+        t_max, t_sum, cross = [], [], []
+        s_sum = jnp.zeros((8, BLOCK), f32)
     for k in range(count):
         part = slice(k * CHUNK, (k + 1) * CHUNK)
-        t = dot_nt(t_left[part, :], t_own)
-        top = jnp.max(t, axis=0, keepdims=True)
-        t = t - top
-        s = dot_nn(s_left[part, :], s_own)
-        te = jnp.exp2(t)
-        se = jnp.exp2(s)
-        t_max.append(top)
-        t_sum.append(jnp.sum(te, axis=0, keepdims=True))
-        cross.append(jnp.sum(te * (t - s), axis=0, keepdims=True))
-        s_sum = s_sum + jnp.sum(se, axis=0, keepdims=True)
-        t_exp[part, :] = te
-        s_exp[part, :] = se
-    top = functools.reduce(jnp.maximum, t_max)
-    lift = [jnp.exp2(x - top) for x in t_max]
-    z = sum(f * x for f, x in zip(lift, t_sum))
-    cross = sum(f * (c + (m - top) * x) for f, c, m, x in zip(lift, cross, t_max, t_sum))
-    kl[...] += math.log(2.0) * cross / z - jnp.log(z) + jnp.log(s_sum)
-    s_gain = LOSS_SCALE / s_sum
-    t_gain = LOSS_SCALE / z
-    x_own = s_feat[:, own]
-    forward = jnp.zeros((SW, BLOCK), f32)
-    for k in range(count):
-        part = slice(k * CHUNK, (k + 1) * CHUNK)
-        grad = (s_exp[part, :] * s_gain - t_exp[part, :] * (t_gain * lift[k])).astype(bf16)
-        forward = forward + dot_nn(s_feat[:, part], grad)
-        total[:, part] += dot_nt(x_own, grad)
-    total[:, own] += forward
+        pieces = [slice(n, n + PIECE) for n in range(k * CHUNK, (k + 1) * CHUNK, PIECE)]
+        if before:
+            t_wide = jnp.concatenate([t_gain[k]] * repeat, axis=0)
+            grad = jnp.concatenate(
+                [(s_exp[n, :] * s_gain - t_exp[n, :] * t_wide).astype(bf16) for n in pieces], axis=0
+            )
+            forward = forward + dot_nn(s_feat[:, part], grad)
+            total[:, part] += dot_nt(x_last, grad)
+        if now:
+            t_all = dot_nt(t_left[part, :], t_own)
+            s_all = dot_nn(s_left[part, :], s_own)
+            top = fold(t_all, jnp.maximum)
+            top_wide = jnp.concatenate([top] * repeat, axis=0)
+            z = jnp.zeros((8, BLOCK), f32)
+            c = jnp.zeros((8, BLOCK), f32)
+            for m, n in enumerate(pieces):
+                t = t_all[m * PIECE : (m + 1) * PIECE, :] - top_wide
+                s = s_all[m * PIECE : (m + 1) * PIECE, :]
+                te = jnp.exp2(t)
+                se = jnp.exp2(s)
+                z = z + fold(te, jnp.add)
+                s_sum = s_sum + fold(se, jnp.add)
+                c = c + fold(te * (t - s), jnp.add)
+                t_exp[n, :] = te
+                s_exp[n, :] = se
+            t_max.append(top)
+            t_sum.append(z)
+            cross.append(c)
+    if before:
+        total[:, last] += forward
+    if now:
+        top = functools.reduce(jnp.maximum, t_max)
+        top = jnp.broadcast_to(jnp.max(top, axis=0, keepdims=True), (8, BLOCK))
+        lift = [jnp.exp2(x - top) for x in t_max]
+        z = sum(f * x for f, x in zip(lift, t_sum))
+        c = sum(f * (c + (m - top) * x) for f, c, m, x in zip(lift, cross, t_max, t_sum))
+        z = jnp.sum(z, axis=0, keepdims=True)
+        c = jnp.sum(c, axis=0, keepdims=True)
+        s_sum = jnp.sum(s_sum, axis=0, keepdims=True)
+        kl[...] += math.log(2.0) * c / z - jnp.log(z) + jnp.log(s_sum)
+        t_gain = jnp.broadcast_to(LOSS_SCALE / z, (8, BLOCK))
+        for k in range(count):
+            gain[k * 8 : k * 8 + 8, :] = t_gain * lift[k]
+        gain[count * 8 :, :] = jnp.broadcast_to(LOSS_SCALE / s_sum, (8, BLOCK))
 
 
 def kernel(
     teacher_hbm, student_hbm, loss_out, grads_out,
     t_in, s_in, t_send, s_send, t_got, s_got, g_send, g_got,
-    t_left, t_right, s_left, s_right, s_feat, t_exp, s_exp, total, kl,
+    t_left, t_right, s_left, s_right, s_feat, t_exp, s_exp, gain, total, kl,
     loss_a, loss_b,
     load_sem, t_send_sem, s_send_sem, g_send_sem, t_got_sem, s_got_sem, g_got_sem, loss_send_sem, loss_got_sem,
 ):
@@ -192,18 +225,23 @@
         wait_blocks(s_got, s_got_sem, r)
         wait_blocks(t_got, t_got_sem, r)
 
-        @pl.when(r < RELATIONS - 1)
+        @pl.when(r == 0)
         def _():
-            send_inputs(r + 1)
+            for n in range(1, RELATIONS):
+                send_inputs(n)
 
         prepare(t_got.at[r], s_got.at[r], t_left, t_right, s_left, s_right, s_feat)
         total[...] = jnp.zeros_like(total)
 
+        refs = (t_left, t_right, s_left, s_right, s_feat, t_exp, s_exp, gain, total, kl)
+
         def step(i, inner):
-            score_block(i, t_left, t_right, s_left, s_right, s_feat, t_exp, s_exp, total, kl)
+            score_step(i, True, True, *refs)
             return inner
 
-        lax.fori_loop(0, LENGTH // BLOCK, step, 0)
+        score_step(0, True, False, *refs)
+        lax.fori_loop(1, LENGTH // BLOCK, step, 0)
+        score_step(LENGTH // BLOCK, False, True, *refs)
         for p in range(DP):
             g_send[r, p] = (total[:, p * ROWS : (p + 1) * ROWS] * (1.0 / math.sqrt(SW))).astype(bf16)
         send_blocks(g_send, g_got, g_send_sem, g_got_sem, r)
@@ -277,6 +315,7 @@
             pltpu.VMEM((SW, LENGTH), bf16),
             pltpu.VMEM((LENGTH, BLOCK), f32),
             pltpu.VMEM((LENGTH, BLOCK), f32),
+            pltpu.VMEM((8 * (LENGTH // CHUNK + 1), BLOCK), f32),
             pltpu.VMEM((SW, LENGTH), f32),
             pltpu.VMEM((1, BLOCK), f32),
             pltpu.VMEM((DP, 8, 128), f32),
@@ -292,7 +331,7 @@
             dma((2,)),
         ],
         compiler_params=pltpu.CompilerParams(
-            collective_id=0, has_side_effects=True, vmem_limit_bytes=48 * 1024 * 1024
+            collective_id=0, has_side_effects=True, vmem_limit_bytes=62 * 1024 * 1024
         ),
     )(teacher_states, student_states)
     return loss[0, 0], grads

time: 80.7 us -> 71.9 us (0.89)
  Pallas kernels: 76.1 us -> 67.6 us
    pallas_call x1, Pallas kernels: 76.1 us -> 67.6 us  [per_device(): pl.pallas_call(kernel, out_shape=(jax.ShapeDtypeStruct((8, 128), f32), ja...]
    unnamed x5 -> x1, local copies, waits for them, and re-layouts: 3.28 us -> 2.28 us
where the time goes in v1:
time: 71.9 us; the launch traced here: 71.7 us
  Pallas kernels  67.6 us (94%)
  local copies, waits for them, and re-layouts  3.47 us (5%)
    pallas_call x1, Pallas kernels, per_device(): pl.pallas_call(kernel, out_shape=(jax.ShapeDtypeStruct((8, 128), f32), ja...  67.6 us
    unnamed x1, local copies, waits for them, and re-layouts  2.28 us

profile of v1, /device:TPU:1, one launch (start us, length us, event | category | flops | bytes accessed | tf_op | source)
XLA Modules:
  0.0 71.7 jit_solution(6977688830850242840)
XLA Ops:
  0.6 67.6 %shard_map.41 = (f32[8,128]{1,0:T(8,128)}, bf16[3,128,2,384]{3,2,1,0:T(2,128)(2,1)}) custom-call(bf16[3,128,2,1024]{3,2,1,0:T(2,128)(2,1)} %teacher_hbm.1, bf16[3,128,2,384]{3,2,1,0:T(2,128)(2,1)} %student_hbm.1), custom_call_target="tpu_custom_call" | custom-call | tf_op jit(solution)/shard_map/pallas_call | solution.py:294
  68.2 1.2 %slice.3 = f32[1,1]{1,0:T(1,128)} slice(f32[8,128]{1,0:T(8,128)} %get-tuple-element.4), slice={[0:1], [0:1]} | slice | bytes 8 | tf_op jit(solution)/shard_map/slice | solution.py:337
  69.4 2.3 %copy.5 = bf16[3,128,2,384]{3,2,1,0:T(2,128)(2,1)} copy(bf16[3,128,2,384]{3,2,1,0:T(2,128)(2,1)} %get-tuple-element.9) | data formatting | bytes 1179648

commit v2 on v1

v2 whole, which is shorter than its diff:
```python
import functools
import math

import jax
import jax.numpy as jnp
from jax import lax
from jax.experimental import pallas as pl
from jax.experimental.pallas import tpu as pltpu
from jax.sharding import PartitionSpec as P

RELATIONS = 3
SEQS = 2
RH = 64
LENGTH = 2048
TW = 128
SW = 48
DP = 16
TENSOR = 8
ROWS = LENGTH // DP
HEADS = RH // TENSOR
BLOCK = 256
BLOCKS = LENGTH // BLOCK
CHUNK = 512
COUNT = LENGTH // CHUNK
PIECE = 32
LOSS_SCALE = 16.0
LOG2E = 1.0 / math.log(2.0)
T_SCALE = LOG2E / math.sqrt(TW)
S_SCALE = LOG2E / math.sqrt(SW)
MESH = pl.DeviceIdType.MESH
f32 = jnp.float32
bf16 = jnp.bfloat16


def dot_nt(a, b):
    return lax.dot_general(a, b, (((1,), (1,)), ((), ())), preferred_element_type=f32)


def dot_nn(a, b):
    return jnp.dot(a, b, preferred_element_type=f32)


def prepare(blocks, t_left, t_right, s_left, s_right, s_feat):
    norms = []
    largest = jnp.zeros((1, ROWS), f32)
    for p in range(DP):
        x = blocks[p, 0:SW, :].astype(f32)
        square = jnp.sum(x * x, axis=0, keepdims=True)
        norms.append(square)
        largest = jnp.maximum(largest, square)
    largest = jnp.max(largest, axis=1, keepdims=True)
    first = lax.broadcasted_iota(jnp.int32, (16, ROWS), 0) == 0
    ones = jnp.where(first, 1.0, 0.0)
    zeros = jnp.zeros((16, ROWS), f32)
    for p in range(DP):
        rows = slice(p * ROWS, (p + 1) * ROWS)
        features = blocks[p, 0:SW, :]
        x = features.astype(f32)
        scaled = x * S_SCALE
        high = scaled.astype(bf16)
        low = (scaled - high.astype(f32)).astype(bf16)
        shift = (0.5 * S_SCALE) * (jnp.sqrt(norms[p] * largest) + norms[p])
        shift = jnp.where(first, -shift, 0.0).astype(bf16)
        s_right[:, rows] = jnp.concatenate([high, low, shift, zeros.astype(bf16)], axis=0)
        s_left[rows, :] = jnp.concatenate([x, x, ones, zeros], axis=0).T.astype(bf16)
        s_feat[:, rows] = features
        x = blocks[p, SW:, :]
        scaled = x.astype(f32) * T_SCALE
        high = scaled.astype(bf16)
        t_left[rows, 0:TW] = x
        t_left[rows, TW:] = x
        t_right[rows, 0:TW] = high
        t_right[rows, TW:] = (scaled - high.astype(f32)).astype(bf16)


def fold(x, op):
    parts = [x[8 * n : 8 * n + 8, :] for n in range(x.shape[0] // 8)]
    while len(parts) > 1:
        parts = [op(*parts[n : n + 2]) if n + 1 < len(parts) else parts[n] for n in range(0, len(parts), 2)]
    return parts[0]


def pipeline_step(scores, exps, grads, work):
    t_raw, s_raw, t_exp, s_exp, t_top, gain, kl = work
    repeat = PIECE // 8
    if grads is not None:
        (s_feat, total), block = grads
        last = pl.ds(pl.multiple_of(block * BLOCK, BLOCK), BLOCK)
        x_last = s_feat[:, last]
        s_gain = jnp.concatenate([gain[COUNT * 8 :, :]] * repeat, axis=0)
        t_gain = [gain[k * 8 : k * 8 + 8, :] for k in range(COUNT)]
        forward = jnp.zeros((SW, BLOCK), f32)
    if exps:
        t_max = [t_top[k * 8 : k * 8 + 8, :] for k in range(COUNT)]
        t_sum, cross = [], []
        s_sum = jnp.zeros((8, BLOCK), f32)
    if scores is not None:
        (t_left, t_right, s_left, s_right), block = scores
        own = pl.ds(pl.multiple_of(block * BLOCK, BLOCK), BLOCK)
        t_own = t_right[own, :]
        s_own = s_right[:, own]
    for k in range(COUNT):
        part = slice(k * CHUNK, (k + 1) * CHUNK)
        pieces = [slice(n, n + PIECE) for n in range(k * CHUNK, (k + 1) * CHUNK, PIECE)]
        if grads is not None:
            t_wide = jnp.concatenate([t_gain[k]] * repeat, axis=0)
            grad = jnp.concatenate(
                [(s_exp[n, :] * s_gain - t_exp[n, :] * t_wide).astype(bf16) for n in pieces], axis=0
            )
            forward = forward + dot_nn(s_feat[:, part], grad)
            total[:, part] += dot_nt(x_last, grad)
        if exps:
            top_wide = jnp.concatenate([t_max[k]] * repeat, axis=0)
            z = jnp.zeros((8, BLOCK), f32)
            c = jnp.zeros((8, BLOCK), f32)
            for n in pieces:
                t = t_raw[n, :] - top_wide
                s = s_raw[n, :]
                te = jnp.exp2(t)
                se = jnp.exp2(s)
                z = z + fold(te, jnp.add)
                s_sum = s_sum + fold(se, jnp.add)
                c = c + fold(te * (t - s), jnp.add)
                t_exp[n, :] = te
                s_exp[n, :] = se
            t_sum.append(z)
            cross.append(c)
        if scores is not None:
            t_all = dot_nt(t_left[part, :], t_own)
            t_raw[part, :] = t_all
            t_top[k * 8 : k * 8 + 8, :] = fold(t_all, jnp.maximum)
            s_raw[part, :] = dot_nn(s_left[part, :], s_own)
    if grads is not None:
        total[:, last] += forward
    if exps:
        top = functools.reduce(jnp.maximum, t_max)
        top = jnp.broadcast_to(jnp.max(top, axis=0, keepdims=True), (8, BLOCK))
        lift = [jnp.exp2(x - top) for x in t_max]
        z = sum(f * x for f, x in zip(lift, t_sum))
        c = sum(f * (c + (m - top) * x) for f, c, m, x in zip(lift, cross, t_max, t_sum))
        z = jnp.sum(z, axis=0, keepdims=True)
        c = jnp.sum(c, axis=0, keepdims=True)
        s_sum = jnp.sum(s_sum, axis=0, keepdims=True)
        kl[...] += math.log(2.0) * c / z - jnp.log(z) + jnp.log(s_sum)
        t_gain = jnp.broadcast_to(LOSS_SCALE / z, (8, BLOCK))
        for k in range(COUNT):
            gain[k * 8 : k * 8 + 8, :] = t_gain * lift[k]
        gain[COUNT * 8 :, :] = jnp.broadcast_to(LOSS_SCALE / s_sum, (8, BLOCK))


def kernel(
    teacher_hbm, student_hbm, loss_out, grads_out,
    t_in, s_in, send, got, g_send, g_got,
    t_left, t_right, s_left, s_right, s_feat, total,
    t_raw, s_raw, t_exp, s_exp, t_top, gain, kl,
    loss_a, loss_b,
    load_sem, send_sem, got_sem, g_send_sem, g_got_sem, loss_send_sem, loss_got_sem,
):
    me = lax.axis_index("dp")
    lane = lax.axis_index("tensor")

    def loads(r):
        return (
            pltpu.make_async_copy(student_hbm.at[r], s_in.at[r], load_sem.at[1, r]),
            pltpu.make_async_copy(teacher_hbm.at[r], t_in.at[r], load_sem.at[0, r]),
        )

    for r in range(RELATIONS):
        for copy in loads(r):
            copy.start()

    barrier = pltpu.get_barrier_semaphore()

    def greet_dp(n, carry):
        pl.semaphore_signal(barrier, inc=1, device_id={"dp": lax.rem(me + n, DP)}, device_id_type=MESH)
        return carry

    def greet_tensor(n, carry):
        pl.semaphore_signal(barrier, inc=1, device_id={"tensor": lax.rem(lane + n, TENSOR)}, device_id_type=MESH)
        return carry

    lax.fori_loop(1, DP, greet_dp, 0)
    lax.fori_loop(1, TENSOR, greet_tensor, 0)

    def pack(r):
        student, teacher = loads(r)
        student.wait()
        for s in range(SEQS):
            x = s_in[r, :, s, :].astype(f32).T.astype(bf16)
            for a in range(HEADS):
                send[r, s * HEADS + a, 0:SW, :] = x[a * SW : (a + 1) * SW, :]
        teacher.wait()
        for s in range(SEQS):
            x = t_in[r, :, s, :]
            for a in range(HEADS):
                send[r, s * HEADS + a, SW:, :] = x[:, a * TW : (a + 1) * TW]

    def send_blocks(source, target, source_sem, target_sem, r):
        def one(n, carry):
            to = lax.rem(me + n, DP)
            pltpu.make_async_remote_copy(
                src_ref=source.at[r, to],
                dst_ref=target.at[r, me],
                send_sem=source_sem.at[r],
                recv_sem=target_sem.at[r],
                device_id={"dp": to},
                device_id_type=MESH,
            ).start()
            return carry

        lax.fori_loop(1, DP, one, 0)
        target[r, me] = source[r, me]

    def wait_blocks(buffer, sem, r):
        span = buffer.at[r, pl.ds(0, DP - 1)]
        pltpu.make_async_copy(span, span, sem.at[r]).wait()

    def place(r):
        wait_blocks(g_got, g_got_sem, r)
        for s in range(SEQS):
            x = g_got[r, s * HEADS : (s + 1) * HEADS].reshape(HEADS * SW, ROWS)
            grads_out[r, :, s, :] = x.T

    def receive(r):
        wait_blocks(got, got_sem, r)
        half = lax.rem(r, 2)
        prepare(got.at[r], t_left.at[half], t_right.at[half], s_left.at[half], s_right.at[half], s_feat.at[half])

    def give_back(r):
        half = lax.rem(r, 2)
        for p in range(DP):
            g_send[r, p] = (total[half, :, p * ROWS : (p + 1) * ROWS] * (1.0 / math.sqrt(SW))).astype(bf16)
        send_blocks(g_send, g_got, g_send_sem, g_got_sem, r)

    def for_scores(n):
        half = lax.rem(n // BLOCKS, 2)
        return (t_left.at[half], t_right.at[half], s_left.at[half], s_right.at[half]), lax.rem(n, BLOCKS)

    def for_grads(n):
        half = lax.rem(n // BLOCKS, 2)
        return (s_feat.at[half], total.at[half]), lax.rem(n, BLOCKS)

    work = (t_raw, s_raw, t_exp, s_exp, t_top, gain, kl)

    pack(0)
    pl.semaphore_wait(barrier, DP - 1 + TENSOR - 1)
    send_blocks(send, got, send_sem, got_sem, 0)
    pack(1)
    pack(2)
    kl[...] = jnp.zeros_like(kl)
    gain[...] = jnp.zeros_like(gain)
    t_exp[...] = jnp.zeros_like(t_exp)
    s_exp[...] = jnp.zeros_like(s_exp)
    s_feat[1] = jnp.zeros_like(s_feat[1])
    total[...] = jnp.zeros_like(total)
    send_blocks(send, got, send_sem, got_sem, 1)
    receive(0)
    pipeline_step(for_scores(0), False, None, work)

    def step(n, carry):
        block = lax.rem(n, BLOCKS)
        r = n // BLOCKS

        @pl.when(n == 0)
        def _():
            send_blocks(send, got, send_sem, got_sem, 2)

        @pl.when((block == BLOCKS - 1) & (r < RELATIONS - 1))
        def _():
            receive(r + 1)

        pipeline_step(for_scores(n + 1), True, for_grads(n + 2 * BLOCKS - 1), work)

        @pl.when((block == 0) & (r > 0))
        def _():
            give_back(r - 1)

        @pl.when((block == 0) & (r < RELATIONS - 1))
        def _():
            half = lax.rem(r + 1, 2)
            total[half] = jnp.zeros((SW, LENGTH), f32)

        return carry

    lax.fori_loop(0, RELATIONS * BLOCKS, step, 0)

    def share(buffer, axis, here, size, which, value):
        buffer[here] = value

        def one(n, carry):
            to = lax.rem(here + n, size)
            pltpu.make_async_remote_copy(
                src_ref=buffer.at[here],
                dst_ref=buffer.at[here],
                send_sem=loss_send_sem.at[which],
                recv_sem=loss_got_sem.at[which],
                device_id={axis: to},
                device_id_type=MESH,
            ).start()
            return carry

        lax.fori_loop(1, size, one, 0)

    def collect(buffer, size, which):
        span = buffer.at[pl.ds(0, size - 1)]
        pltpu.make_async_copy(span, span, loss_got_sem.at[which]).wait()
        return functools.reduce(lambda a, b: a + b, [buffer[n] for n in range(size)])

    part = jnp.broadcast_to(jnp.sum(kl[...], axis=1, keepdims=True), (8, 128))
    share(loss_a, "dp", me, DP, 0, part)
    pipeline_step(None, False, for_grads(RELATIONS * BLOCKS - 1), work)
    give_back(RELATIONS - 1)
    share(loss_b, "tensor", lane, TENSOR, 1, collect(loss_a, DP, 0))
    for r in range(RELATIONS - 1):
        place(r)
    loss_out[...] = collect(loss_b, TENSOR, 1) * (1.0 / (RELATIONS * SEQS * RH * LENGTH))
    for r in range(RELATIONS):
        wait_blocks(send, send_sem, r)
        wait_blocks(g_send, g_send_sem, r)
    for which, buffer, size in ((0, loss_a, DP), (1, loss_b, TENSOR)):
        span = buffer.at[pl.ds(0, size - 1)]
        pltpu.make_async_copy(span, span, loss_send_sem.at[which]).wait()
    place(RELATIONS - 1)


def per_device(teacher_states, student_states):
    dma = pltpu.SemaphoreType.DMA
    loss, grads = pl.pallas_call(
        kernel,
        out_shape=(
            jax.ShapeDtypeStruct((8, 128), f32),
            jax.ShapeDtypeStruct(student_states.shape, bf16),
        ),
        in_specs=[pl.BlockSpec(memory_space=pl.ANY)] * 2,
        out_specs=(pl.BlockSpec(memory_space=pltpu.VMEM), pl.BlockSpec(memory_space=pltpu.VMEM)),
        scratch_shapes=[
            pltpu.VMEM((RELATIONS, ROWS, SEQS, HEADS * TW), bf16),
            pltpu.VMEM((RELATIONS, ROWS, SEQS, HEADS * SW), bf16),
            pltpu.VMEM((RELATIONS, DP, SW + ROWS, 128), bf16),
            pltpu.VMEM((RELATIONS, DP, SW + ROWS, 128), bf16),
            pltpu.VMEM((RELATIONS, DP, SW, ROWS), bf16),
            pltpu.VMEM((RELATIONS, DP, SW, ROWS), bf16),
            pltpu.VMEM((2, LENGTH, 2 * TW), bf16),
            pltpu.VMEM((2, LENGTH, 2 * TW), bf16),
            pltpu.VMEM((2, LENGTH, 128), bf16),
            pltpu.VMEM((2, 128, LENGTH), bf16),
            pltpu.VMEM((2, SW, LENGTH), bf16),
            pltpu.VMEM((2, SW, LENGTH), f32),
            pltpu.VMEM((LENGTH, BLOCK), f32),
            pltpu.VMEM((LENGTH, BLOCK), f32),
            pltpu.VMEM((LENGTH, BLOCK), f32),
            pltpu.VMEM((LENGTH, BLOCK), f32),
            pltpu.VMEM((8 * COUNT, BLOCK), f32),
            pltpu.VMEM((8 * (COUNT + 1), BLOCK), f32),
            pltpu.VMEM((1, BLOCK), f32),
            pltpu.VMEM((DP, 8, 128), f32),
            pltpu.VMEM((TENSOR, 8, 128), f32),
            dma((2, RELATIONS)),
            dma((RELATIONS,)),
            dma((RELATIONS,)),
            dma((RELATIONS,)),
            dma((RELATIONS,)),
            dma((2,)),
            dma((2,)),
        ],
        compiler_params=pltpu.CompilerParams(
            collective_id=0, has_side_effects=True, vmem_limit_bytes=54000 * 1024
        ),
    )(teacher_states, student_states)
    return loss[0, 0], grads


def solution(mesh):
    placed = (P(None, "dp", None, "tensor"), P(None, "dp", None, "tensor"))
    return jax.shard_map(
        per_device,
        mesh=mesh,
        in_specs=placed,
        out_specs=(P(), P(None, "dp", None, "tensor")),
        check_vma=False,
    )
```

time: 71.9 us -> 67.8 us (0.943)
  Pallas kernels: 67.6 us -> 64.6 us
  local copies, waits for them, and re-layouts: 3.47 us -> 2.38 us
    pallas_call x1, Pallas kernels: 67.6 us -> 64.6 us  [per_device(): pl.pallas_call(kernel, out_shape=(jax.ShapeDtypeStruct((8, 128), f32), ja...]
    unnamed x1 -> x3, local copies, waits for them, and re-layouts: 2.28 us -> 1.87 us
where the time goes in v2:
time: 67.8 us; the launch traced here: 67.6 us
  Pallas kernels  64.6 us (95%)
  local copies, waits for them, and re-layouts  2.38 us (4%)
    pallas_call x1, Pallas kernels, per_device(): pl.pallas_call(kernel, out_shape=(jax.ShapeDtypeStruct((8, 128), f32), ja...  64.6 us
    unnamed x3, local copies, waits for them, and re-layouts  1.87 us

profile of v2, /device:TPU:1, one launch (start us, length us, event | category | flops | bytes accessed | tf_op | source)
XLA Modules:
  0.0 67.6 jit_solution(17277984253366467546)
XLA Ops:
  0.6 0.0 copy-start
  0.6 1.1 %copy-done = bf16[3,128,2,384]{3,2,1,0:T(2,128)(2,1)S(1)} copy-done((bf16[3,128,2,384]{3,2,1,0:T(2,128)(2,1)S(1)}, bf16[3,128,2,384]{3,2,1,0:T(2,128)(2,1)}, u32[]{:S(2)}) %copy-start) | copy-done | bytes 589848
  1.7 64.6 %shard_map.41 = (f32[8,128]{1,0:T(8,128)S(1)}, bf16[3,128,2,384]{3,2,1,0:T(2,128)(2,1)S(1)}) custom-call(bf16[3,128,2,1024]{3,2,1,0:T(2,128)(2,1)} %teacher_hbm.1, bf16[3,128,2,384]{3,2,1,0:T(2,128)(2,1)S(1)} %copy-done), custom_call_target="tpu_custom_call" | custom-call | tf_op jit(solution)/shard_map/pallas_call | solution.py:328
  66.3 0.5 slice.3
  66.8 0.8 %copy.5 = bf16[3,128,2,384]{3,2,1,0:T(2,128)(2,1)} copy(bf16[3,128,2,384]{3,2,1,0:T(2,128)(2,1)S(1)} %get-tuple-element.9) | data formatting | bytes 1179648
Async XLA Ops:
  0.6 1.1 %copy-start = (bf16[3,128,2,384]{3,2,1,0:T(2,128)(2,1)S(1)}, bf16[3,128,2,384]{3,2,1,0:T(2,128)(2,1)}, u32[]{:S(2)}) copy-start(bf16[3,128,2,384]{3,2,1,0:T(2,128)(2,1)} %student_hbm.1) | copy-start | bytes 1769476

commit v3 on v2

--- a/solution.py
+++ b/solution.py
@@ -226,10 +226,12 @@
         half = lax.rem(r, 2)
         prepare(got.at[r], t_left.at[half], t_right.at[half], s_left.at[half], s_right.at[half], s_feat.at[half])
 
-    def give_back(r):
+    def round_grads(r):
         half = lax.rem(r, 2)
         for p in range(DP):
             g_send[r, p] = (total[half, :, p * ROWS : (p + 1) * ROWS] * (1.0 / math.sqrt(SW))).astype(bf16)
+
+    def give_back(r):
         send_blocks(g_send, g_got, g_send_sem, g_got_sem, r)
 
     def for_scores(n):
@@ -273,6 +275,7 @@
 
         @pl.when((block == 0) & (r > 0))
         def _():
+            round_grads(r - 1)
             give_back(r - 1)
 
         @pl.when((block == 0) & (r < RELATIONS - 1))
@@ -282,7 +285,8 @@
 
         return carry
 
-    lax.fori_loop(0, RELATIONS * BLOCKS, step, 0)
+    lax.fori_loop(0, RELATIONS * BLOCKS - 1, step, 0)
+    pipeline_step(None, True, for_grads(RELATIONS * BLOCKS - 2), work)
 
     def share(buffer, axis, here, size, which, value):
         buffer[here] = value
@@ -309,8 +313,9 @@
     part = jnp.broadcast_to(jnp.sum(kl[...], axis=1, keepdims=True), (8, 128))
     share(loss_a, "dp", me, DP, 0, part)
     pipeline_step(None, False, for_grads(RELATIONS * BLOCKS - 1), work)
+    round_grads(RELATIONS - 1)
+    share(loss_b, "tensor", lane, TENSOR, 1, collect(loss_a, DP, 0))
     give_back(RELATIONS - 1)
-    share(loss_b, "tensor", lane, TENSOR, 1, collect(loss_a, DP, 0))
     for r in range(RELATIONS - 1):
         place(r)
     loss_out[...] = collect(loss_b, TENSOR, 1) * (1.0 / (RELATIONS * SEQS * RH * LENGTH))
@@ -364,7 +369,7 @@
             dma((2,)),
         ],
         compiler_params=pltpu.CompilerParams(
-            collective_id=0, has_side_effects=True, vmem_limit_bytes=54000 * 1024
+            collective_id=0, has_side_effects=True, vmem_limit_bytes=54400 * 1024
         ),
     )(teacher_states, student_states)
     return loss[0, 0], grads

time: 67.8 us -> 66.2 us (0.976)
  local copies, waits for them, and re-layouts: 2.38 us -> 1.33 us
    unnamed x3 -> x1, local copies, waits for them, and re-layouts: 1.87 us -> 0.81 us
where the time goes in v3:
time: 66.2 us; the launch traced here: 66 us
  Pallas kernels  64.1 us (97%)
  local copies, waits for them, and re-layouts  1.33 us (2%)
    pallas_call x1, Pallas kernels, per_device(): pl.pallas_call(kernel, out_shape=(jax.ShapeDtypeStruct((8, 128), f32), ja...  64.1 us

profile of v3, /device:TPU:1, one launch (start us, length us, event | category | flops | bytes accessed | tf_op | source)
XLA Modules:
  0.0 66.0 jit_solution(11896921969513676471)
XLA Ops:
  0.6 64.1 %shard_map.41 = (f32[8,128]{1,0:T(8,128)S(1)}, bf16[3,128,2,384]{3,2,1,0:T(2,128)(2,1)S(1)}) custom-call(bf16[3,128,2,1024]{3,2,1,0:T(2,128)(2,1)} %teacher_hbm.1, bf16[3,128,2,384]{3,2,1,0:T(2,128)(2,1)} %student_hbm.1), custom_call_target="tpu_custom_call" | custom-call | tf_op jit(solution)/shard_map/pallas_call | solution.py:333
  64.7 0.5 slice.3
  65.2 0.8 %copy.5 = bf16[3,128,2,384]{3,2,1,0:T(2,128)(2,1)} copy(bf16[3,128,2,384]{3,2,1,0:T(2,128)(2,1)S(1)} %get-tuple-element.9) | data formatting | bytes 1179648

commit v4 on v3

--- a/solution.py
+++ b/solution.py
@@ -182,46 +182,53 @@
     lax.fori_loop(1, DP, greet_dp, 0)
     lax.fori_loop(1, TENSOR, greet_tensor, 0)
 
-    def pack(r):
-        student, teacher = loads(r)
-        student.wait()
-        for s in range(SEQS):
-            x = s_in[r, :, s, :].astype(f32).T.astype(bf16)
-            for a in range(HEADS):
-                send[r, s * HEADS + a, 0:SW, :] = x[a * SW : (a + 1) * SW, :]
-        teacher.wait()
-        for s in range(SEQS):
-            x = t_in[r, :, s, :]
-            for a in range(HEADS):
-                send[r, s * HEADS + a, SW:, :] = x[:, a * TW : (a + 1) * TW]
-
-    def send_blocks(source, target, source_sem, target_sem, r):
+    def pack(r, s):
+        x = s_in[r, :, s, :].astype(f32).T.astype(bf16)
+        for a in range(HEADS):
+            send[r, SEQS * a + s, 0:SW, :] = x[a * SW : (a + 1) * SW, :]
+        x = t_in[r, :, s, :]
+        for a in range(HEADS):
+            send[r, SEQS * a + s, SW:, :] = x[:, a * TW : (a + 1) * TW]
+
+    def send_one(source, target, source_sem, target_sem, r, to):
+        pltpu.make_async_remote_copy(
+            src_ref=source.at[r, to],
+            dst_ref=target.at[r, me],
+            send_sem=source_sem.at[r],
+            recv_sem=target_sem.at[r],
+            device_id={"dp": to},
+            device_id_type=MESH,
+        ).start()
+
+    def send_blocks(source, target, source_sem, target_sem, r, low=1, high=DP):
         def one(n, carry):
-            to = lax.rem(me + n, DP)
-            pltpu.make_async_remote_copy(
-                src_ref=source.at[r, to],
-                dst_ref=target.at[r, me],
-                send_sem=source_sem.at[r],
-                recv_sem=target_sem.at[r],
-                device_id={"dp": to},
-                device_id_type=MESH,
-            ).start()
+            send_one(source, target, source_sem, target_sem, r, lax.rem(me + n, DP))
             return carry
 
-        lax.fori_loop(1, DP, one, 0)
-        target[r, me] = source[r, me]
+        lax.fori_loop(low, high, one, 0)
+
+    def send_half(r, s):
+        odd = lax.rem(me + s, SEQS)
+
+        def one(n, carry):
+            send_one(send, got, send_sem, got_sem, r, lax.rem(me + odd + SEQS * n, DP))
+            return carry
+
+        lax.fori_loop(1 - odd, HEADS, one, 0)
 
     def wait_blocks(buffer, sem, r):
         span = buffer.at[r, pl.ds(0, DP - 1)]
         pltpu.make_async_copy(span, span, sem.at[r]).wait()
 
     def place(r):
+        g_got[r, me] = g_send[r, me]
         wait_blocks(g_got, g_got_sem, r)
         for s in range(SEQS):
-            x = g_got[r, s * HEADS : (s + 1) * HEADS].reshape(HEADS * SW, ROWS)
+            x = jnp.concatenate([g_got[r, SEQS * a + s] for a in range(HEADS)], axis=0)
             grads_out[r, :, s, :] = x.T
 
     def receive(r):
+        got[r, me] = send[r, me]
         wait_blocks(got, got_sem, r)
         half = lax.rem(r, 2)
         prepare(got.at[r], t_left.at[half], t_right.at[half], s_left.at[half], s_right.at[half], s_feat.at[half])
@@ -231,8 +238,8 @@
         for p in range(DP):
             g_send[r, p] = (total[half, :, p * ROWS : (p + 1) * ROWS] * (1.0 / math.sqrt(SW))).astype(bf16)
 
-    def give_back(r):
-        send_blocks(g_send, g_got, g_send_sem, g_got_sem, r)
+    def give_back(r, low=1, high=DP):
+        send_blocks(g_send, g_got, g_send_sem, g_got_sem, r, low, high)
 
     def for_scores(n):
         half = lax.rem(n // BLOCKS, 2)
@@ -244,11 +251,18 @@
 
     work = (t_raw, s_raw, t_exp, s_exp, t_top, gain, kl)
 
-    pack(0)
+    for copy in loads(0):
+        copy.wait()
+    pack(0, 0)
     pl.semaphore_wait(barrier, DP - 1 + TENSOR - 1)
-    send_blocks(send, got, send_sem, got_sem, 0)
-    pack(1)
-    pack(2)
+    send_half(0, 0)
+    pack(0, 1)
+    send_half(0, 1)
+    for r in range(1, RELATIONS):
+        for copy in loads(r):
+            copy.wait()
+        for s in range(SEQS):
+            pack(r, s)
     kl[...] = jnp.zeros_like(kl)
     gain[...] = jnp.zeros_like(gain)
     t_exp[...] = jnp.zeros_like(t_exp)
@@ -314,8 +328,9 @@
     share(loss_a, "dp", me, DP, 0, part)
     pipeline_step(None, False, for_grads(RELATIONS * BLOCKS - 1), work)
     round_grads(RELATIONS - 1)
+    give_back(RELATIONS - 1, 1, DP // 2)
     share(loss_b, "tensor", lane, TENSOR, 1, collect(loss_a, DP, 0))
-    give_back(RELATIONS - 1)
+    give_back(RELATIONS - 1, DP // 2, DP)
     for r in range(RELATIONS - 1):
         place(r)
     loss_out[...] = collect(loss_b, TENSOR, 1) * (1.0 / (RELATIONS * SEQS * RH * LENGTH))

time: 66.2 us -> 65.5 us (0.989)
  Pallas kernels: 64.1 us -> 63.4 us
where the time goes in v4:
time: 65.5 us; the launch traced here: 65.4 us
  Pallas kernels  63.4 us (97%)
  local copies, waits for them, and re-layouts  1.33 us (2%)
    pallas_call x1, Pallas kernels, per_device(): pl.pallas_call(kernel, out_shape=(jax.ShapeDtypeStruct((8, 128), f32), ja...  63.4 us

profile of v4, /device:TPU:1, one launch (start us, length us, event | category | flops | bytes accessed | tf_op | source)
XLA Modules:
  0.0 65.4 jit_solution(10520565203901160126)
XLA Ops:
  0.6 63.4 %shard_map.41 = (f32[8,128]{1,0:T(8,128)S(1)}, bf16[3,128,2,384]{3,2,1,0:T(2,128)(2,1)S(1)}) custom-call(bf16[3,128,2,1024]{3,2,1,0:T(2,128)(2,1)} %teacher_hbm.1, bf16[3,128,2,384]{3,2,1,0:T(2,128)(2,1)} %student_hbm.1), custom_call_target="tpu_custom_call" | custom-call | tf_op jit(solution)/shard_map/pallas_call | solution.py:348
  64.1 0.5 slice.3
  64.6 0.8 %copy.5 = bf16[3,128,2,384]{3,2,1,0:T(2,128)(2,1)} copy(bf16[3,128,2,384]{3,2,1,0:T(2,128)(2,1)S(1)} %get-tuple-element.9) | data formatting | bytes 1179648

commit v5 on v4

--- a/solution.py
+++ b/solution.py
@@ -269,7 +269,6 @@
     s_exp[...] = jnp.zeros_like(s_exp)
     s_feat[1] = jnp.zeros_like(s_feat[1])
     total[...] = jnp.zeros_like(total)
-    send_blocks(send, got, send_sem, got_sem, 1)
     receive(0)
     pipeline_step(for_scores(0), False, None, work)
 
@@ -277,9 +276,11 @@
         block = lax.rem(n, BLOCKS)
         r = n // BLOCKS
 
-        @pl.when(n == 0)
-        def _():
-            send_blocks(send, got, send_sem, got_sem, 2)
+        for r_next, at in ((1, 0), (2, 5)):
+
+            @pl.when(n == at)
+            def _():
+                send_blocks(send, got, send_sem, got_sem, r_next)
 
         @pl.when((block == BLOCKS - 1) & (r < RELATIONS - 1))
         def _():

time: 65.5 us -> 68.8 us (1.050)
  Pallas kernels: 63.4 us -> 66.7 us
    pallas_call x1, Pallas kernels: 63.4 us -> 66.7 us  [per_device(): pl.pallas_call(kernel, out_shape=(jax.ShapeDtypeStruct((8, 128), f32), ja...]
where the time goes in v5:
time: 68.8 us; the launch traced here: 68.7 us
  Pallas kernels  66.7 us (97%)
  local copies, waits for them, and re-layouts  1.33 us (2%)
    pallas_call x1, Pallas kernels, per_device(): pl.pallas_call(kernel, out_shape=(jax.ShapeDtypeStruct((8, 128), f32), ja...  66.7 us

profile of v5, /device:TPU:1, one launch (start us, length us, event | category | flops | bytes accessed | tf_op | source)
XLA Modules:
  0.0 68.7 jit_solution(3470300847999472646)
XLA Ops:
  0.6 66.7 %shard_map.41 = (f32[8,128]{1,0:T(8,128)S(1)}, bf16[3,128,2,384]{3,2,1,0:T(2,128)(2,1)S(1)}) custom-call(bf16[3,128,2,1024]{3,2,1,0:T(2,128)(2,1)} %teacher_hbm.1, bf16[3,128,2,384]{3,2,1,0:T(2,128)(2,1)} %student_hbm.1), custom_call_target="tpu_custom_call" | custom-call | tf_op jit(solution)/shard_map/pallas_call | solution.py:349
  67.4 0.5 slice.3
  67.9 0.8 %copy.5 = bf16[3,128,2,384]{3,2,1,0:T(2,128)(2,1)} copy(bf16[3,128,2,384]{3,2,1,0:T(2,128)(2,1)S(1)} %get-tuple-element.9) | data formatting | bytes 1179648

commit v6 on v4

--- a/solution.py
+++ b/solution.py
@@ -263,13 +263,14 @@
             copy.wait()
         for s in range(SEQS):
             pack(r, s)
+            if r == 1:
+                send_half(r, s)
     kl[...] = jnp.zeros_like(kl)
     gain[...] = jnp.zeros_like(gain)
     t_exp[...] = jnp.zeros_like(t_exp)
     s_exp[...] = jnp.zeros_like(s_exp)
     s_feat[1] = jnp.zeros_like(s_feat[1])
     total[...] = jnp.zeros_like(total)
-    send_blocks(send, got, send_sem, got_sem, 1)
     receive(0)
     pipeline_step(for_scores(0), False, None, work)
 

time: 65.5 us -> 65.5 us (level)
  no operation moved by 1% of the time
where the time goes in v6:
time: 65.5 us; the launch traced here: 65.4 us
  Pallas kernels  63.4 us (97%)
  local copies, waits for them, and re-layouts  1.33 us (2%)
    pallas_call x1, Pallas kernels, per_device(): pl.pallas_call(kernel, out_shape=(jax.ShapeDtypeStruct((8, 128), f32), ja...  63.4 us

profile of v6, /device:TPU:1, one launch (start us, length us, event | category | flops | bytes accessed | tf_op | source)
XLA Modules:
  0.0 65.4 jit_solution(12825679727817720027)
XLA Ops:
  0.6 63.4 %shard_map.41 = (f32[8,128]{1,0:T(8,128)S(1)}, bf16[3,128,2,384]{3,2,1,0:T(2,128)(2,1)S(1)}) custom-call(bf16[3,128,2,1024]{3,2,1,0:T(2,128)(2,1)} %teacher_hbm.1, bf16[3,128,2,384]{3,2,1,0:T(2,128)(2,1)} %student_hbm.1), custom_call_target="tpu_custom_call" | custom-call | tf_op jit(solution)/shard_map/pallas_call | solution.py:349
  64.1 0.5 slice.3
  64.6 0.8 %copy.5 = bf16[3,128,2,384]{3,2,1,0:T(2,128)(2,1)} copy(bf16[3,128,2,384]{3,2,1,0:T(2,128)(2,1)S(1)} %get-tuple-element.9) | data formatting | bytes 1179648

commit v7 on v5

--- a/solution.py
+++ b/solution.py
@@ -263,6 +263,7 @@
             copy.wait()
         for s in range(SEQS):
             pack(r, s)
+            send_half(r, s)
     kl[...] = jnp.zeros_like(kl)
     gain[...] = jnp.zeros_like(gain)
     t_exp[...] = jnp.zeros_like(t_exp)
@@ -275,12 +276,6 @@
     def step(n, carry):
         block = lax.rem(n, BLOCKS)
         r = n // BLOCKS
-
-        for r_next, at in ((1, 0), (2, 5)):
-
-            @pl.when(n == at)
-            def _():
-                send_blocks(send, got, send_sem, got_sem, r_next)
 
         @pl.when((block == BLOCKS - 1) & (r < RELATIONS - 1))
         def _():

time: 68.8 us -> 65.3 us (0.949)
  Pallas kernels: 66.7 us -> 63.2 us
    pallas_call x1, Pallas kernels: 66.7 us -> 63.2 us  [per_device(): pl.pallas_call(kernel, out_shape=(jax.ShapeDtypeStruct((8, 128), f32), ja...]
where the time goes in v7:
time: 65.3 us; the launch traced here: 65.2 us
  Pallas kernels  63.2 us (97%)
  local copies, waits for them, and re-layouts  1.33 us (2%)
    pallas_call x1, Pallas kernels, per_device(): pl.pallas_call(kernel, out_shape=(jax.ShapeDtypeStruct((8, 128), f32), ja...  63.2 us

profile of v7, /device:TPU:1, one launch (start us, length us, event | category | flops | bytes accessed | tf_op | source)
XLA Modules:
  0.0 65.2 jit_solution(9450652410536711535)
XLA Ops:
  0.6 63.2 %shard_map.41 = (f32[8,128]{1,0:T(8,128)S(1)}, bf16[3,128,2,384]{3,2,1,0:T(2,128)(2,1)S(1)}) custom-call(bf16[3,128,2,1024]{3,2,1,0:T(2,128)(2,1)} %teacher_hbm.1, bf16[3,128,2,384]{3,2,1,0:T(2,128)(2,1)} %student_hbm.1), custom_call_target="tpu_custom_call" | custom-call | tf_op jit(solution)/shard_map/pallas_call | solution.py:344
  63.8 0.5 slice.3
  64.4 0.8 %copy.5 = bf16[3,128,2,384]{3,2,1,0:T(2,128)(2,1)} copy(bf16[3,128,2,384]{3,2,1,0:T(2,128)(2,1)S(1)} %get-tuple-element.9) | data formatting | bytes 1179648

commit v8 on v7

--- a/solution.py
+++ b/solution.py
@@ -22,7 +22,7 @@
 BLOCKS = LENGTH // BLOCK
 CHUNK = 512
 COUNT = LENGTH // CHUNK
-PIECE = 32
+PIECE = 16
 LOSS_SCALE = 16.0
 LOG2E = 1.0 / math.log(2.0)
 T_SCALE = LOG2E / math.sqrt(TW)
@@ -330,13 +330,13 @@
     for r in range(RELATIONS - 1):
         place(r)
     loss_out[...] = collect(loss_b, TENSOR, 1) * (1.0 / (RELATIONS * SEQS * RH * LENGTH))
+    place(RELATIONS - 1)
     for r in range(RELATIONS):
         wait_blocks(send, send_sem, r)
         wait_blocks(g_send, g_send_sem, r)
     for which, buffer, size in ((0, loss_a, DP), (1, loss_b, TENSOR)):
         span = buffer.at[pl.ds(0, size - 1)]
         pltpu.make_async_copy(span, span, loss_send_sem.at[which]).wait()
-    place(RELATIONS - 1)
 
 
 def per_device(teacher_states, student_states):

time: 65.3 us -> 65.1 us (level)
  no operation moved by 1% of the time
where the time goes in v8:
time: 65.1 us; the launch traced here: 64.9 us
  Pallas kernels  63 us (97%)
  local copies, waits for them, and re-layouts  1.33 us (2%)
    pallas_call x1, Pallas kernels, per_device(): pl.pallas_call(kernel, out_shape=(jax.ShapeDtypeStruct((8, 128), f32), ja...  63 us

profile of v8, /device:TPU:1, one launch (start us, length us, event | category | flops | bytes accessed | tf_op | source)
XLA Modules:
  0.0 64.9 jit_solution(7607105363723631008)
XLA Ops:
  0.6 63.0 %shard_map.41 = (f32[8,128]{1,0:T(8,128)S(1)}, bf16[3,128,2,384]{3,2,1,0:T(2,128)(2,1)S(1)}) custom-call(bf16[3,128,2,1024]{3,2,1,0:T(2,128)(2,1)} %teacher_hbm.1, bf16[3,128,2,384]{3,2,1,0:T(2,128)(2,1)} %student_hbm.1), custom_call_target="tpu_custom_call" | custom-call | tf_op jit(solution)/shard_map/pallas_call | solution.py:344
  63.6 0.5 slice.3
  64.1 0.8 %copy.5 = bf16[3,128,2,384]{3,2,1,0:T(2,128)(2,1)} copy(bf16[3,128,2,384]{3,2,1,0:T(2,128)(2,1)S(1)} %get-tuple-element.9) | data formatting | bytes 1179648
